TPU v7x, 32 devices: a whole 2x2x4 slice. The times are simulated.
32 devices in a mesh: groups: 2 (over x), aux: 16 (over z, y, core).
Axes of the slice: x: 2, y: 2, z: 4, core: 2. Of those that a mesh axis runs over, the one named last changes fastest.
Arguments:
- integrals: bfloat16 [1024, 256, 256], P(('groups', 'aux')), parts along dimension 0, may hold values from -6 to 6
- coeffs: bfloat16 [512, 256], P('groups'), parts along dimension 0, may hold values from -0.375 to 0.375
- metric_inverse: bfloat16 [1024, 512], P('groups'), parts along dimension 0, may hold values from -3 to 3, as said below
- screen: int32 [8, 2, 2], P('groups'), parts along dimension 0, may hold values 0 or 1
Outputs:
- exchange: float32 [512, 256], P(('groups', 'aux')), parts along dimension 0
There are 2 independent parts, one for each index of `groups`. A program takes and returns all parts, laid end to end along the dimension named above; each array names one. Nothing has to cross between parts.
Inputs may be any that keep to these rules, and one draw needn't show every extreme that they name: `metric_inverse`: symmetric, with diagonal entries between 0.5 and 2 and off-diagonal entries of size about 0.35·√2/√512; it is not guaranteed positive definite.
All inputs are finite; a program needn't handle non-finite values.
Results may differ from a plain program's by a relative error of at most 0.00033.
Values may be sent and summed in bfloat16 or wider, within the bound.
A program may use at most 128 MiB of HBM per device.

v0:
```python
import math

import jax
import jax.numpy as jnp
from jax import lax
from jax.sharding import PartitionSpec as P

TILE = 128


def contract_with_metric(metric_inverse, block):
    fitted_tensor = jnp.einsum(
        "pq,iqm->ipm", metric_inverse, block, preferred_element_type=jnp.float32
    )
    return fitted_tensor.astype(jnp.bfloat16)


def contribution(left, right, scale_factor):
    term = lax.dot_general(
        left, right, (((0, 1), (0, 1)), ((), ())), preferred_element_type=jnp.float32
    )
    return term * scale_factor


def local(integrals, coeffs, metric_inverse, screen):
    auxiliary_subset = integrals.shape[0]
    basis = integrals.shape[1]
    occupied = coeffs.shape[1]
    tile_count = screen.shape[0]
    leading_row = lax.axis_index("aux") * auxiliary_subset
    row_tiles = (leading_row + jnp.arange(auxiliary_subset, dtype=jnp.int32)) // TILE
    selector_matrix = (
        row_tiles[:, None] == jnp.arange(tile_count, dtype=jnp.int32)[None, :]
    ).astype(jnp.float32)
    row_flags = jnp.einsum("uw,wje->euj", selector_matrix, screen.astype(jnp.float32))
    product = lax.dot_general(
        coeffs, integrals, (((0,), (2,)), ((), ())), preferred_element_type=jnp.float32
    )
    product = product.reshape(occupied // TILE, TILE, auxiliary_subset, basis // TILE, TILE)
    product = product * row_flags[:, None, :, :, None]
    half = product.reshape(occupied, auxiliary_subset, basis).astype(jnp.bfloat16)
    moved = lax.all_to_all(half, "aux", split_axis=0, concat_axis=1, tiled=True)
    fitted_tensor = contract_with_metric(metric_inverse, moved)
    scale_factor = 1.0 / math.sqrt(moved.shape[1] * occupied)
    partial_sum = contribution(moved, fitted_tensor, scale_factor)
    return lax.psum_scatter(partial_sum, "aux", scatter_dimension=0, tiled=True)


def solution(mesh):
    in_specs = (
        P(("groups", "aux"), None, None),
        P("groups", None),
        P("groups", None),
        P("groups", None, None),
    )
    out_specs = P(("groups", "aux"), None)
    return jax.shard_map(local, mesh=mesh, in_specs=in_specs, out_specs=out_specs, check_vma=False)
```

profile of v0, /device:TPU:0, one launch (start us, length us, event | category | flops | bytes accessed | tf_op | source)
XLA Modules:
  0.0 206.5 jit_solution(6695236955884938660)
XLA Ops:
  6.5 0.0 copy-start
  6.5 0.0 reduce-scatter.2.cloned.1.call-start
  6.6 0.7 convert_element_type.13
  7.3 0.1 fusion.14
  7.4 0.1 copy.19
  7.5 5.5 %mul.21 = f32[2,128,32,2,128]{4,3,1,0,2:T(2,128)} broadcast(f32[2,32,2]{2,0,1:T(2,128)S(1)} %copy.19), dimensions={0,2,3} | broadcast | bytes 8389120 | tf_op jit(solution)/shard_map/mul | solution.py:40
  13.0 0.0 copy-start.1
  13.0 11.5 %mul.22 = f32[256,32,256]{2,0,1:T(8,128)} reshape(f32[2,128,32,2,128]{4,3,1,0,2:T(2,128)} %mul.21) | data formatting | bytes 16777216 | tf_op jit(solution)/shard_map/mul | solution.py:40
  24.5 0.0 copy-done.1
  24.5 6.0 %multiply_convert_fusion = bf16[256,32,256]{2,0,1:T(8,128)(2,1)S(1)} fusion(f32[256,32,256]{2,0,1:T(8,128)} %mul.22, bf16[32,256,256]{2,1,0:T(8,128)(2,1)} %param.4, bf16[256,256]{1,0:T(8,128)(2,1)S(1)} %copy-done.1), kind=kOutput, calls=%fused_computation | convolution fusion | flops 1077936128 | bytes 16908288 | tf_op jit(solution)/shard_map/dot_general | solution.py:36
  30.5 2.4 %copy.20 = bf16[256,32,256]{2,1,0:T(8,128)(2,1)S(1)} copy(bf16[256,32,256]{2,0,1:T(8,128)(2,1)S(1)} %multiply_convert_fusion) | data formatting | bytes 8388608 | tf_op jit(solution)/shard_map/convert_element_type | solution.py:41
  32.9 99.4 %all_to_all.18 = bf16[256,32,256]{2,1,0:T(8,128)(2,1)S(1)} all-to-all(bf16[256,32,256]{2,1,0:T(8,128)(2,1)S(1)} %copy.20), channel_id=1, replica_groups=mesh['groups'=2,'aux'=16] {'aux'}, dimensions={0} | all-to-all | bytes 8388608 | tf_op jit(solution)/shard_map/all_to_all | solution.py:42
  132.4 2.4 %copy.21 = bf16[16,16,32,256]{3,2,1,0:T(8,128)(2,1)} copy(bf16[16,16,32,256]{3,2,0,1:T(8,128)(2,1)S(1)} %bitcast.32) | data formatting | bytes 8388608 | tf_op jit(solution)/shard_map/all_to_all | solution.py:42
  134.8 0.0 copy-done
  134.8 8.8 %fusion.8 = f32[256,256]{1,0:T(8,128)} fusion(bf16[16,512,256]{2,1,0:T(8,128)(2,1)} %bitcast.33, bf16[512,512]{1,0:T(8,128)(2,1)S(1)} %copy-done), kind=kOutput, calls=%fused_computation.6 | convolution fusion | flops 3223388160 | bytes 4980736 | tf_op jit(solution)/shard_map/dot_general | solution.py:19
  143.6 0.0 reduce-scatter.2.cloned.1.call-update
  143.6 56.1 %reduce-scatter.2.cloned.1.call-done = f32[16,256]{1,0:T(8,128)} async-done(((f32[256,256]{1,0:T(8,128)}), f32[16,256]{1,0:T(8,128)}) %reduce-scatter.2.cloned.1.call-update) | async-done | bytes 16400 | tf_op jit(solution)/shard_map/reduce_scatter | solution.py:46
  (2 shorter events, 0.0 us)
Async XLA Ops:
  6.5 128.2 %copy-start = (bf16[512,512]{1,0:T(8,128)(2,1)S(1)}, bf16[512,512]{1,0:T(8,128)(2,1)}, u32[]{:S(2)}) copy-start(bf16[512,512]{1,0:T(8,128)(2,1)} %param.6) | copy-start | bytes 1572868
  6.5 193.2 %reduce-scatter.2.cloned.1.call-start = ((), (), s32[]{:S(2)}) async-start(), calls=%async_computation.2 | async-start | bytes 278528 | tf_op jit(solution)/shard_map/reduce_scatter | solution.py:46
  13.0 11.5 %copy-start.1 = (bf16[256,256]{1,0:T(8,128)(2,1)S(1)}, bf16[256,256]{1,0:T(8,128)(2,1)}, u32[]{:S(2)}) copy-start(bf16[256,256]{1,0:T(8,128)(2,1)} %param.5) | copy-start | bytes 393220
Sparse Core Ops, SparseCore 0:
  143.7 55.9 reduce-scatter.1
where the time goes:
time: 207 us
  blocking collectives  99.4 us (48%)
  waiting for transfers between devices  56.1 us (27%)
  local copies, waits for them, and re-layouts  21.9 us (11%)
  matrix products  14.9 us (7%)
  between operations  13.4 us (6%)
    all_to_all x1, blocking collectives, local(): moved = lax.all_to_all(half, 'aux', split_axis=0, concat_axis=1, tiled=True)  99.4 us
    reduce_scatter x1, waiting for transfers between devices, local(): return lax.psum_scatter(partial_sum, 'aux', scatter_dimension=0, tiled=True)  56.1 us
    mul x2, local copies, waits for them, and re-layouts, local(): product = product * row_flags[:, None, :, :, None]  17 us
    dot_general x1, matrix products, contribution(): lax.dot_general(left, right, (((0, 1), (0, 1)), ((), ())), preferred_elem...  8.82 us
    dot_general x1, matrix products, local(): lax.dot_general(coeffs, integrals, (((0,), (2,)), ((), ())), preferred_el...  5.97 us
  transfers between devices with their start and end apart: 1, of which 1 were waited for; matrix products, arithmetic and copies ran while one was open for 0% of the time, Pallas kernels for 0%

commit v1 on v0

v1 whole, which is shorter than its diff:
```python
import functools
import math

import jax
import jax.numpy as jnp
from jax import lax
from jax.experimental import pallas as pl
from jax.experimental.pallas import tpu as pltpu
from jax.sharding import PartitionSpec as P

TILE = 128
GROUP = 16
MESH = pl.DeviceIdType.MESH


def peer(me, step, n):
    offset = n // 2 + ((step + 1) // 2) * (1 - 2 * (step % 2))
    return lax.rem(me + offset, n)


def kernel(
    n, chunk, integrals_hbm, coeffs_hbm, metric_hbm, screen_ref, out_ref,
    integrals, coeffs, coeffs_t, metric, stage, half, landed, total, blocks, parts,
    load_sem, send_sem, recv_sem, part_send_sem, part_recv_sem,
):
    me = lax.axis_index("aux")
    rows, basis, _ = integrals.shape
    occupied = coeffs.shape[1]
    aux = metric.shape[0]
    groups = rows // GROUP
    mine = occupied // n
    chunks = mine // chunk
    out_rows = basis // n
    scale = 1.0 / math.sqrt(aux * occupied)

    coeffs_copy = pltpu.make_async_copy(coeffs_hbm, coeffs, load_sem.at[0])
    metric_copy = pltpu.make_async_copy(metric_hbm, metric, load_sem.at[1])
    integral_copies = [
        pltpu.make_async_copy(
            integrals_hbm.at[pl.ds(g * GROUP, GROUP)],
            integrals.at[pl.ds(g * GROUP, GROUP)],
            load_sem.at[2 + g],
        )
        for g in range(groups)
    ]
    coeffs_copy.start()
    for copy in integral_copies:
        copy.start()
    metric_copy.start()

    barrier = pltpu.get_barrier_semaphore()

    @pl.loop(0, n - 1)
    def _(step):
        pl.semaphore_signal(
            barrier, inc=1, device_id={"aux": peer(me, step, n)}, device_id_type=MESH
        )

    tile = me * rows // TILE
    flags = [
        [screen_ref[tile, mt, it].astype(jnp.float32) for it in range(occupied // TILE)]
        for mt in range(basis // TILE)
    ]
    coeffs_copy.wait()
    coeffs_t[...] = coeffs[...].T

    def source(group, first, count, owner):
        return half.at[group, pl.ds(owner * mine + first, count)]

    def target(group, first, count, owner):
        start = pl.multiple_of(owner * rows + group * GROUP, GROUP)
        return landed.at[pl.ds(first, count), pl.ds(start, GROUP)]

    def transfer(unit, group, first, count, to, owner):
        return pltpu.make_async_remote_copy(
            src_ref=source(group, first, count, to),
            dst_ref=target(group, first, count, owner),
            send_sem=send_sem.at[unit, to],
            recv_sem=recv_sem.at[unit, owner],
            device_id={"aux": to},
            device_id_type=MESH,
        )

    units = [(g, 0, mine) for g in range(groups - 1)]
    units += [(groups - 1, c * chunk, chunk) for c in range(chunks)]

    for g in range(groups):
        integral_copies[g].wait()

        @pl.loop(0, GROUP)
        def _(p):
            product = lax.dot_general(
                coeffs_t[...], integrals[g * GROUP + p],
                (((1,), (1,)), ((), ())), preferred_element_type=jnp.float32,
            )
            for it in range(occupied // TILE):
                for mt in range(basis // TILE):
                    stage[mt, pl.ds(it * TILE * GROUP + p, TILE, stride=GROUP), :] = (
                        product[it * TILE:(it + 1) * TILE, mt * TILE:(mt + 1) * TILE] * flags[mt][it]
                    )

        def convert(owner):
            first = pl.multiple_of(owner * (mine * GROUP), mine * GROUP)
            block = stage[:, pl.ds(first, mine * GROUP), :].astype(jnp.bfloat16)
            return [part.reshape(mine, GROUP, TILE) for part in block]

        if g == 0:
            pl.semaphore_wait(barrier, n - 1)
        mine_units = [(u, unit) for u, unit in enumerate(units) if unit[0] == g]
        for index, (u, (_, first, count)) in enumerate(mine_units):
            @pl.loop(0, n - 1)
            def _(step):
                to = peer(me, step, n)
                if index == 0:
                    for mt, part in enumerate(convert(to)):
                        half[g, pl.ds(to * mine, mine), :, mt * TILE:(mt + 1) * TILE] = part
                transfer(u, g, first, count, to, me).start()

        start = pl.multiple_of(me * rows + g * GROUP, GROUP)
        for mt, part in enumerate(convert(me)):
            landed[:, pl.ds(start, GROUP), mt * TILE:(mt + 1) * TILE] = part

    metric_copy.wait()
    total[...] = jnp.zeros_like(total)

    def contract(i):
        depth = min(aux, 512)

        @pl.loop(0, aux // depth)
        def _(b):
            first = pl.multiple_of(b * depth, depth)
            fitted = jnp.dot(
                metric[pl.ds(first, depth), :], landed[i], preferred_element_type=jnp.float32
            ).astype(jnp.bfloat16)
            total[...] += lax.dot_general(
                landed[i, pl.ds(first, depth), :], fitted,
                (((0,), (0,)), ((), ())), preferred_element_type=jnp.float32,
            )

    for u, (g, first, count) in enumerate(units):
        @pl.loop(0, n - 1)
        def _(step):
            owner = peer(me, step, n)
            transfer(u, g, first, count, owner, owner).wait_recv()

        if g == groups - 1:
            pl.loop(first, first + count)(contract)

    for d in range(n):
        blocks[d] = total[d * out_rows:(d + 1) * out_rows, :]

    def part_transfer(to, owner):
        return pltpu.make_async_remote_copy(
            src_ref=blocks.at[to],
            dst_ref=parts.at[owner],
            send_sem=part_send_sem.at[to],
            recv_sem=part_recv_sem.at[owner],
            device_id={"aux": to},
            device_id_type=MESH,
        )

    @pl.loop(0, n - 1)
    def _(step):
        part_transfer(peer(me, step, n), me).start()

    parts[me] = blocks[me]

    @pl.loop(0, n - 1)
    def _(step):
        owner = peer(me, step, n)
        part_transfer(owner, owner).wait_recv()

    out_ref[...] = jnp.sum(parts[...], axis=0) * scale

    for u, (g, first, count) in enumerate(units):
        @pl.loop(0, n - 1)
        def _(step):
            to = peer(me, step, n)
            transfer(u, g, first, count, to, me).wait_send()

    @pl.loop(0, n - 1)
    def _(step):
        part_transfer(peer(me, step, n), me).wait_send()


def local(n, integrals, coeffs, metric_inverse, screen):
    rows, basis, _ = integrals.shape
    occupied = coeffs.shape[1]
    aux = metric_inverse.shape[0]
    mine = occupied // n
    chunk = min(4, mine)
    groups = rows // GROUP
    units = groups - 1 + mine // chunk
    out_rows = basis // n
    return pl.pallas_call(
        functools.partial(kernel, n, chunk),
        out_shape=jax.ShapeDtypeStruct((out_rows, basis), jnp.float32),
        in_specs=[pl.BlockSpec(memory_space=pl.ANY)] * 3 + [pl.BlockSpec(memory_space=pltpu.SMEM)],
        out_specs=pl.BlockSpec(memory_space=pltpu.VMEM),
        scratch_shapes=[
            pltpu.VMEM(integrals.shape, jnp.bfloat16),
            pltpu.VMEM(coeffs.shape, jnp.bfloat16),
            pltpu.VMEM((occupied, basis), jnp.bfloat16),
            pltpu.VMEM(metric_inverse.shape, jnp.bfloat16),
            pltpu.VMEM((basis // TILE, occupied * GROUP, TILE), jnp.float32),
            pltpu.VMEM((groups, occupied, GROUP, basis), jnp.bfloat16),
            pltpu.VMEM((mine, aux, basis), jnp.bfloat16),
            pltpu.VMEM((basis, basis), jnp.float32),
            pltpu.VMEM((n, out_rows, basis), jnp.float32),
            pltpu.VMEM((n, out_rows, basis), jnp.float32),
            pltpu.SemaphoreType.DMA((2 + groups,)),
            pltpu.SemaphoreType.DMA((units, n)),
            pltpu.SemaphoreType.DMA((units, n)),
            pltpu.SemaphoreType.DMA((n,)),
            pltpu.SemaphoreType.DMA((n,)),
        ],
        compiler_params=pltpu.CompilerParams(
            collective_id=0, has_side_effects=True, vmem_limit_bytes=48 * 1024 * 1024
        ),
        cost_estimate=pl.CostEstimate(
            flops=2 * basis * occupied * (rows * basis + aux * (aux + basis) // n),
            bytes_accessed=2 * (rows * basis * basis + aux * aux + basis * occupied),
            transcendentals=0,
        ),
    )(integrals, coeffs, metric_inverse, screen)


def solution(mesh):
    in_specs = (
        P(("groups", "aux"), None, None),
        P("groups", None),
        P("groups", None),
        P("groups", None, None),
    )
    out_specs = P(("groups", "aux"), None)
    return jax.shard_map(
        functools.partial(local, mesh.shape["aux"]),
        mesh=mesh, in_specs=in_specs, out_specs=out_specs, check_vma=False,
    )
```

time: 207 us -> 118 us (0.57)
  Pallas kernels: 0 us -> 113 us
  blocking collectives: 99.4 us -> 0 us
  waiting for transfers between devices: 56.1 us -> 0 us
  local copies, waits for them, and re-layouts: 21.9 us -> 5.51 us
  matrix products: 14.9 us -> 0 us
  between operations: 13.4 us -> 0.01 us
    pallas_call x0 -> x1, Pallas kernels: none -> 113 us  [local(): pl.pallas_call(functools.partial(kernel, n, chunk), out_shape=jax.ShapeDt...]
    all_to_all x1 -> x0, blocking collectives: 99.4 us -> none  [local(): moved = lax.all_to_all(half, 'aux', split_axis=0, concat_axis=1, tiled=True)]
    reduce_scatter x1 -> x0, waiting for transfers between devices: 56.1 us -> none  [local(): return lax.psum_scatter(partial_sum, 'aux', scatter_dimension=0, tiled=True)]
    mul x2 -> x0, local copies, waits for them, and re-layouts: 17 us -> none  [local(): product = product * row_flags[:, None, :, :, None]]
    dot_general x2 -> x0, matrix products: 14.8 us -> none  [the longest x1 8.82 us: contribution(): lax.dot_general(left, right, (((0, 1), (0, 1)), ((), ())), preferred_elem...]
    unnamed x4 -> x8, local copies, waits for them, and re-layouts: 0.01 us -> 5.51 us
    convert_element_type x1 -> x0, local copies, waits for them, and re-layouts: 2.44 us -> none  [local(): product.reshape(occupied, auxiliary_subset, basis).astype(jnp.bfloat16)]
    all_to_all x1 -> x0, local copies, waits for them, and re-layouts: 2.37 us -> none  [local(): moved = lax.all_to_all(half, 'aux', split_axis=0, concat_axis=1, tiled=True)]
  transfers between devices with their start and end apart: 1 -> 0, of which waited for: 1 -> 0; matrix products, arithmetic and copies ran while one was open for 0% -> 0% of each run, Pallas kernels for 0% -> 0%
where the time goes in v1:
time: 118 us
  Pallas kernels  113 us (96%)
  local copies, waits for them, and re-layouts  5.51 us (5%)
    pallas_call x1, Pallas kernels, local(): pl.pallas_call(functools.partial(kernel, n, chunk), out_shape=jax.ShapeDt...  113 us
    unnamed x8, local copies, waits for them, and re-layouts  5.51 us

profile of v1, /device:TPU:0, one launch (start us, length us, event | category | flops | bytes accessed | tf_op | source)
XLA Modules:
  0.0 118.2 jit_solution(3194785951548620537)
XLA Ops:
  0.0 0.8 copy.5.screen_ref
  0.8 0.0 copy-start
  0.8 2.2 %copy-done = bf16[32,256,256]{2,1,0:T(8,128)(2,1)S(1)} copy-done((bf16[32,256,256]{2,1,0:T(8,128)(2,1)S(1)}, bf16[32,256,256]{2,1,0:T(8,128)(2,1)}, u32[]{:S(2)}) %copy-start) | copy-done | bytes 4194328
  3.0 0.0 copy-start.1
  3.0 1.0 copy-done.1
  4.0 0.0 copy-start.2
  4.0 0.9 copy-done.2
  4.9 112.7 %shard_map.46 = f32[16,256]{1,0:T(8,128)S(1)} custom-call(bf16[32,256,256]{2,1,0:T(8,128)(2,1)S(1)} %copy-done, bf16[256,256]{1,0:T(8,128)(2,1)S(1)} %copy-done.2, bf16[512,512]{1,0:T(8,128)(2,1)S(1)} %copy-done.1, s32[4,2,2]{2,1,0:T(2,128)S(1)} %copy.5.screen_ref), custom_call_target="tpu_custom_call" | custom-call | flops 4294967296 | bytes 4849664 | tf_op jit(solution)/shard_map/pallas_call | solution.py:195
  117.6 0.6 copy.7
Async XLA Ops:
  0.8 2.2 %copy-start = (bf16[32,256,256]{2,1,0:T(8,128)(2,1)S(1)}, bf16[32,256,256]{2,1,0:T(8,128)(2,1)}, u32[]{:S(2)}) copy-start(bf16[32,256,256]{2,1,0:T(8,128)(2,1)} %integrals_hbm.1) | copy-start | bytes 12582916
  3.0 1.0 copy-start.1
  4.0 0.9 copy-start.2

commit v2 on v1

--- a/solution.py
+++ b/solution.py
@@ -14,14 +14,13 @@
 
 
 def peer(me, step, n):
-    offset = n // 2 + ((step + 1) // 2) * (1 - 2 * (step % 2))
-    return lax.rem(me + offset, n)
+    return lax.rem(me + step + 1, n)
 
 
 def kernel(
-    n, chunk, integrals_hbm, coeffs_hbm, metric_hbm, screen_ref, out_ref,
-    integrals, coeffs, coeffs_t, metric, stage, half, landed, total, blocks, parts,
-    load_sem, send_sem, recv_sem, part_send_sem, part_recv_sem,
+    n, chunks, integrals_hbm, coeffs_hbm, metric_hbm, screen_ref, out_ref,
+    integrals, coeffs, coeffs_t, metric, stage, half, landed, total, blocks, sibling_blocks, sums, parts,
+    load_sem, send_sem, recv_sem, pair_send_sem, pair_recv_sem, part_send_sem, part_recv_sem,
 ):
     me = lax.axis_index("aux")
     rows, basis, _ = integrals.shape
@@ -29,7 +28,6 @@
     aux = metric.shape[0]
     groups = rows // GROUP
     mine = occupied // n
-    chunks = mine // chunk
     out_rows = basis // n
     scale = 1.0 / math.sqrt(aux * occupied)
 
@@ -58,7 +56,7 @@
 
     tile = me * rows // TILE
     flags = [
-        [screen_ref[tile, mt, it].astype(jnp.float32) for it in range(occupied // TILE)]
+        [screen_ref[mt, it, tile].astype(jnp.float32) for it in range(occupied // TILE)]
         for mt in range(basis // TILE)
     ]
     coeffs_copy.wait()
@@ -68,8 +66,7 @@
         return half.at[group, pl.ds(owner * mine + first, count)]
 
     def target(group, first, count, owner):
-        start = pl.multiple_of(owner * rows + group * GROUP, GROUP)
-        return landed.at[pl.ds(first, count), pl.ds(start, GROUP)]
+        return landed.at[owner * groups + group, pl.ds(first, count)]
 
     def transfer(unit, group, first, count, to, owner):
         return pltpu.make_async_remote_copy(
@@ -82,12 +79,12 @@
         )
 
     units = [(g, 0, mine) for g in range(groups - 1)]
-    units += [(groups - 1, c * chunk, chunk) for c in range(chunks)]
+    units += [(groups - 1, first, count) for first, count in chunks]
 
     for g in range(groups):
         integral_copies[g].wait()
 
-        @pl.loop(0, GROUP)
+        @pl.loop(0, GROUP, unroll=4)
         def _(p):
             product = lax.dot_general(
                 coeffs_t[...], integrals[g * GROUP + p],
@@ -116,9 +113,8 @@
                         half[g, pl.ds(to * mine, mine), :, mt * TILE:(mt + 1) * TILE] = part
                 transfer(u, g, first, count, to, me).start()
 
-        start = pl.multiple_of(me * rows + g * GROUP, GROUP)
         for mt, part in enumerate(convert(me)):
-            landed[:, pl.ds(start, GROUP), mt * TILE:(mt + 1) * TILE] = part
+            landed[me * groups + g, :, :, mt * TILE:(mt + 1) * TILE] = part
 
     metric_copy.wait()
     total[...] = jnp.zeros_like(total)
@@ -130,10 +126,10 @@
         def _(b):
             first = pl.multiple_of(b * depth, depth)
             fitted = jnp.dot(
-                metric[pl.ds(first, depth), :], landed[i], preferred_element_type=jnp.float32
+                metric[pl.ds(first, depth), :], landed[:, i].reshape(aux, basis), preferred_element_type=jnp.float32
             ).astype(jnp.bfloat16)
             total[...] += lax.dot_general(
-                landed[i, pl.ds(first, depth), :], fitted,
+                landed[pl.ds(first // GROUP, depth // GROUP), i].reshape(depth, basis), fitted,
                 (((0,), (0,)), ((), ())), preferred_element_type=jnp.float32,
             )
 
@@ -144,30 +140,43 @@
             transfer(u, g, first, count, owner, owner).wait_recv()
 
         if g == groups - 1:
-            pl.loop(first, first + count)(contract)
-
+            pl.loop(first, first + count, unroll=min(count, 4))(contract)
+
+    core, chip = lax.rem(me, 2), me // 2
+    chips = n // 2
     for d in range(n):
-        blocks[d] = total[d * out_rows:(d + 1) * out_rows, :]
+        blocks[d % 2, d // 2] = total[d * out_rows:(d + 1) * out_rows, :]
+    pair = pltpu.make_async_remote_copy(
+        src_ref=blocks.at[1 - core],
+        dst_ref=sibling_blocks,
+        send_sem=pair_send_sem,
+        recv_sem=pair_recv_sem,
+        device_id={"aux": me + 1 - 2 * core},
+        device_id_type=MESH,
+    )
+    pair.start()
+    pair.wait_recv()
+    sums[...] = blocks[core] + sibling_blocks[...]
 
     def part_transfer(to, owner):
         return pltpu.make_async_remote_copy(
-            src_ref=blocks.at[to],
+            src_ref=sums.at[to],
             dst_ref=parts.at[owner],
             send_sem=part_send_sem.at[to],
             recv_sem=part_recv_sem.at[owner],
-            device_id={"aux": to},
+            device_id={"aux": 2 * to + core},
             device_id_type=MESH,
         )
 
-    @pl.loop(0, n - 1)
-    def _(step):
-        part_transfer(peer(me, step, n), me).start()
-
-    parts[me] = blocks[me]
-
-    @pl.loop(0, n - 1)
-    def _(step):
-        owner = peer(me, step, n)
+    @pl.loop(0, chips - 1)
+    def _(step):
+        part_transfer(peer(chip, step, chips), chip).start()
+
+    parts[chip] = sums[chip]
+
+    @pl.loop(0, chips - 1)
+    def _(step):
+        owner = peer(chip, step, chips)
         part_transfer(owner, owner).wait_recv()
 
     out_ref[...] = jnp.sum(parts[...], axis=0) * scale
@@ -178,9 +187,11 @@
             to = peer(me, step, n)
             transfer(u, g, first, count, to, me).wait_send()
 
-    @pl.loop(0, n - 1)
-    def _(step):
-        part_transfer(peer(me, step, n), me).wait_send()
+    pair.wait_send()
+
+    @pl.loop(0, chips - 1)
+    def _(step):
+        part_transfer(peer(chip, step, chips), chip).wait_send()
 
 
 def local(n, integrals, coeffs, metric_inverse, screen):
@@ -188,12 +199,13 @@
     occupied = coeffs.shape[1]
     aux = metric_inverse.shape[0]
     mine = occupied // n
-    chunk = min(4, mine)
+    tail = max(mine // 4, 1)
+    chunks = [(0, mine - tail), (mine - tail, tail)]
     groups = rows // GROUP
-    units = groups - 1 + mine // chunk
+    units = groups - 1 + len(chunks)
     out_rows = basis // n
     return pl.pallas_call(
-        functools.partial(kernel, n, chunk),
+        functools.partial(kernel, n, chunks),
         out_shape=jax.ShapeDtypeStruct((out_rows, basis), jnp.float32),
         in_specs=[pl.BlockSpec(memory_space=pl.ANY)] * 3 + [pl.BlockSpec(memory_space=pltpu.SMEM)],
         out_specs=pl.BlockSpec(memory_space=pltpu.VMEM),
@@ -204,25 +216,29 @@
             pltpu.VMEM(metric_inverse.shape, jnp.bfloat16),
             pltpu.VMEM((basis // TILE, occupied * GROUP, TILE), jnp.float32),
             pltpu.VMEM((groups, occupied, GROUP, basis), jnp.bfloat16),
-            pltpu.VMEM((mine, aux, basis), jnp.bfloat16),
+            pltpu.VMEM((aux // GROUP, mine, GROUP, basis), jnp.bfloat16),
             pltpu.VMEM((basis, basis), jnp.float32),
-            pltpu.VMEM((n, out_rows, basis), jnp.float32),
-            pltpu.VMEM((n, out_rows, basis), jnp.float32),
+            pltpu.VMEM((2, n // 2, out_rows, basis), jnp.float32),
+            pltpu.VMEM((n // 2, out_rows, basis), jnp.float32),
+            pltpu.VMEM((n // 2, out_rows, basis), jnp.float32),
+            pltpu.VMEM((n // 2, out_rows, basis), jnp.float32),
             pltpu.SemaphoreType.DMA((2 + groups,)),
             pltpu.SemaphoreType.DMA((units, n)),
             pltpu.SemaphoreType.DMA((units, n)),
-            pltpu.SemaphoreType.DMA((n,)),
-            pltpu.SemaphoreType.DMA((n,)),
+            pltpu.SemaphoreType.DMA,
+            pltpu.SemaphoreType.DMA,
+            pltpu.SemaphoreType.DMA((n // 2,)),
+            pltpu.SemaphoreType.DMA((n // 2,)),
         ],
         compiler_params=pltpu.CompilerParams(
-            collective_id=0, has_side_effects=True, vmem_limit_bytes=48 * 1024 * 1024
+            collective_id=0, has_side_effects=True, vmem_limit_bytes=60 * 1024 * 1024
         ),
         cost_estimate=pl.CostEstimate(
             flops=2 * basis * occupied * (rows * basis + aux * (aux + basis) // n),
             bytes_accessed=2 * (rows * basis * basis + aux * aux + basis * occupied),
             transcendentals=0,
         ),
-    )(integrals, coeffs, metric_inverse, screen)
+    )(integrals, coeffs, metric_inverse, jnp.transpose(screen, (1, 2, 0)))
 
 
 def solution(mesh):

time: 118 us -> 109 us (0.924)
  Pallas kernels: 113 us -> 108 us
  local copies, waits for them, and re-layouts: 5.51 us -> 1.32 us
    pallas_call x1, Pallas kernels: 113 us -> 108 us  [local(): pl.pallas_call(functools.partial(kernel, n, chunks), out_shape=jax.ShapeD...]
    unnamed x8 -> x1, local copies, waits for them, and re-layouts: 5.51 us -> 1.32 us
where the time goes in v2:
time: 109 us
  Pallas kernels  108 us (99%)
  local copies, waits for them, and re-layouts  1.32 us (1%)
    pallas_call x1, Pallas kernels, local(): pl.pallas_call(functools.partial(kernel, n, chunks), out_shape=jax.ShapeD...  108 us

profile of v2, /device:TPU:0, one launch (start us, length us, event | category | flops | bytes accessed | tf_op | source)
XLA Modules:
  0.0 109.1 jit_solution(16205399156804544741)
XLA Ops:
  0.0 107.8 %shard_map.46 = f32[16,256]{1,0:T(8,128)} custom-call(bf16[32,256,256]{2,1,0:T(8,128)(2,1)} %integrals_hbm.1, bf16[256,256]{1,0:T(8,128)(2,1)} %coeffs_hbm.1, bf16[512,512]{1,0:T(8,128)(2,1)} %metric_hbm.1, s32[2,2,4]{2,1,0:T(2,128)} %bitcast.1), custom_call_target="tpu_custom_call" | custom-call | flops 4294967296 | bytes 4849664 | tf_op jit(solution)/shard_map/pallas_call | solution.py:207
  107.8 1.3 %copy.6 = f32[16,256]{1,0:T(8,128)} copy(f32[16,256]{1,0:T(8,128)} %shard_map.46) | data formatting | bytes 32768

commit v3 on v2

--- a/solution.py
+++ b/solution.py
@@ -102,13 +102,19 @@
             return [part.reshape(mine, GROUP, TILE) for part in block]
 
         if g == 0:
+            @pl.loop(0, n - 1)
+            def _(step):
+                to = peer(me, step, n)
+                for mt, part in enumerate(convert(to)):
+                    half[g, pl.ds(to * mine, mine), :, mt * TILE:(mt + 1) * TILE] = part
+
             pl.semaphore_wait(barrier, n - 1)
         mine_units = [(u, unit) for u, unit in enumerate(units) if unit[0] == g]
         for index, (u, (_, first, count)) in enumerate(mine_units):
             @pl.loop(0, n - 1)
             def _(step):
                 to = peer(me, step, n)
-                if index == 0:
+                if index == 0 and g > 0:
                     for mt, part in enumerate(convert(to)):
                         half[g, pl.ds(to * mine, mine), :, mt * TILE:(mt + 1) * TILE] = part
                 transfer(u, g, first, count, to, me).start()

time: 109 us -> 110 us (level)
  no operation moved by 1% of the time
where the time goes in v3:
time: 110 us; the launch traced here: 109 us
  Pallas kernels  108 us (98%)
  local copies, waits for them, and re-layouts  1.32 us (1%)
    pallas_call x1, Pallas kernels, local(): pl.pallas_call(functools.partial(kernel, n, chunks), out_shape=jax.ShapeD...  108 us

profile of v3, /device:TPU:0, one launch (start us, length us, event | category | flops | bytes accessed | tf_op | source)
XLA Modules:
  0.0 109.4 jit_solution(9132156556511667693)
XLA Ops:
  0.0 108.1 %shard_map.46 = f32[16,256]{1,0:T(8,128)} custom-call(bf16[32,256,256]{2,1,0:T(8,128)(2,1)} %integrals_hbm.1, bf16[256,256]{1,0:T(8,128)(2,1)} %coeffs_hbm.1, bf16[512,512]{1,0:T(8,128)(2,1)} %metric_hbm.1, s32[2,2,4]{2,1,0:T(2,128)} %bitcast.1), custom_call_target="tpu_custom_call" | custom-call | flops 4294967296 | bytes 4849664 | tf_op jit(solution)/shard_map/pallas_call | solution.py:213
  108.1 1.3 %copy.6 = f32[16,256]{1,0:T(8,128)} copy(f32[16,256]{1,0:T(8,128)} %shard_map.46) | data formatting | bytes 32768
